TPU v7x, 512 devices: a whole 4x4x16 slice. The times are simulated.
512 devices in a mesh: gx: 32 (over y, x, z_hi), gy: 16 (over z_lo, core).
Axes of the slice: x: 4, y: 4, z: 16 (z_hi: 2, z_lo: 8; z = z_hi * 8 + z_lo), core: 2. Of those that a mesh axis runs over, the one named last changes fastest.
Arguments:
- picture_embedding_matrix: bfloat16 [262144, 1152], P(('gx', 'gy')), may hold values from -6 to 6
- caption_embedding_matrix: bfloat16 [262144, 1152], P(('gx', 'gy')), may hold values from -6 to 6
- score_scale: float32 [1], replicated, may hold values from 10 to 40
- logit_offset: float32 [1], replicated, may hold values from -4 to -1
Outputs:
- row_loss: float32 [262144], P(('gx', 'gy'))
- image_grad: bfloat16 [262144, 1152], P(('gx', 'gy'))
- text_grad: bfloat16 [262144, 1152], P(('gx', 'gy'))
All inputs are finite; a program needn't handle non-finite values.
Results may differ from a plain program's by a relative error of at most 0.0074.
Values may be sent and summed in bfloat16 or wider, within the bound.
A program may use at most 64 MiB of HBM per device.

v0:
```python
import jax
import jax.numpy as jnp
from jax import lax
from jax.sharding import PartitionSpec as P


def passed_along(block, axis, distance):
    devices = range(lax.axis_size(axis))
    route = [((i - distance) % len(devices), i) for i in devices]
    return lax.ppermute(block, axis, route)


def normalize(raw):
    wide = raw.astype(jnp.float32)
    inverse = lax.rsqrt(jnp.sum(wide * wide, axis=-1, keepdims=True) + 1e-06)
    return ((wide * inverse).astype(jnp.bfloat16), inverse, wide * inverse)


def couple_weight(
    picture_tile_entries, caption_tile_entries, matching_couple, score_scale, logit_offset
):
    couple_scores = (
        score_scale[0]
        * jnp.dot(picture_tile_entries, caption_tile_entries.T, preferred_element_type=jnp.float32)
        + logit_offset[0]
    )
    count = couple_scores.shape[0]
    same = jnp.arange(count)[:, None] == jnp.arange(count)[None, :]
    match_polarity = jnp.where(jnp.logical_and(same, matching_couple), 1.0, -1.0).astype(
        jnp.float32
    )
    block_losses = jnp.sum(jax.nn.softplus(-match_polarity * couple_scores), axis=1)
    objective_weight = (
        -score_scale[0] * match_polarity * jax.nn.sigmoid(-match_polarity * couple_scores)
    ).astype(jnp.bfloat16)
    return (block_losses, objective_weight)


def backnorm(inverse, unit, direction):
    return (
        inverse * (direction - unit * jnp.sum(unit * direction, axis=-1, keepdims=True))
    ).astype(jnp.bfloat16)


def narrow_term(objective_weight, block):
    return jnp.dot(objective_weight.T, block, preferred_element_type=jnp.float32).astype(
        jnp.bfloat16
    )


def body(picture_embedding_matrix, caption_embedding_matrix, score_scale, logit_offset):
    picture_unit_vectors, inv_img, img_unit = normalize(picture_embedding_matrix)
    txt_n, inv_txt, txt_unit = normalize(caption_embedding_matrix)
    rows_here = picture_embedding_matrix.shape[0]
    txt_gx = passed_along(txt_n, "gx", 1)
    txt_gy, txt_both = passed_along((txt_n, txt_gx), "gy", 1)
    met_list = ((txt_n, True), (txt_gx, False), (txt_gy, False), (txt_both, False))
    loss_sum = jnp.zeros((rows_here,), jnp.float32)
    img_dir = jnp.zeros(picture_embedding_matrix.shape, jnp.float32)
    coefs = []
    for covered_couples, matching_couple in met_list:
        block_losses, objective_weight = couple_weight(
            picture_unit_vectors, covered_couples, matching_couple, score_scale, logit_offset
        )
        loss_sum = loss_sum + block_losses
        img_dir = img_dir + jnp.dot(
            objective_weight, covered_couples, preferred_element_type=jnp.float32
        )
        coefs.append(objective_weight)
    own_term = jnp.dot(coefs[0].T, picture_unit_vectors, preferred_element_type=jnp.float32)
    term_gx = narrow_term(coefs[1], picture_unit_vectors)
    term_gy = narrow_term(coefs[2], picture_unit_vectors)
    term_both = narrow_term(coefs[3], picture_unit_vectors)
    back_own, back_gx = passed_along((term_gy, term_both), "gy", -1)
    back_first, back_second = passed_along((term_gx, back_gx), "gx", -1)
    txt_dir = (
        own_term
        + back_own.astype(jnp.float32)
        + back_first.astype(jnp.float32)
        + back_second.astype(jnp.float32)
    )
    row_loss = loss_sum / (4.0 * rows_here)
    image_grad = backnorm(inv_img, img_unit, img_dir)
    text_grad = backnorm(inv_txt, txt_unit, txt_dir)
    return (row_loss, image_grad, text_grad)


def solution(mesh):
    return jax.shard_map(
        body,
        mesh=mesh,
        in_specs=(P(("gx", "gy"), None), P(("gx", "gy"), None), P(), P()),
        out_specs=(P(("gx", "gy")), P(("gx", "gy"), None), P(("gx", "gy"), None)),
        check_vma=False,
    )
```

profile of v0, /device:TPU:7, one launch (start us, length us, event | category | flops | bytes accessed | tf_op | source)
XLA Modules:
  0.0 407.6 jit_solution(5726310678794550208)
XLA Ops:
  0.6 0.0 copy-start
  0.6 1.7 fusion.15
  2.3 0.0 copy-done
  2.3 0.0 copy-start.1
  2.3 0.3 fusion.2
  2.6 15.6 %collective-permute-start = (bf16[512,1152]{1,0:T(8,128)(2,1)S(1)}, bf16[512,1152]{1,0:T(8,128)(2,1)}, u32[]{:S(2)}, u32[]{:S(2)}) collective-permute-start(bf16[512,1152]{1,0:T(8,128)(2,1)S(1)} %fusion.2), channel_id=1, source_target_pairs={{496,0},{0,16},{16,32},{32,48},{48,64},{64,80},{80,96},{96,112},{1... | collective-permute-start | bytes 3538952 | tf_op jit(solution)/shard_map/ppermute | solution.py:10
  18.2 3.5 collective-permute-start.1
  23.0 0.0 copy-done.1
  23.0 0.3 fusion.10
  23.3 2.5 fusion.23
  25.8 37.1 %collective-permute-done = bf16[512,1152]{1,0:T(8,128)(2,1)} collective-permute-done((bf16[512,1152]{1,0:T(8,128)(2,1)S(1)}, bf16[512,1152]{1,0:T(8,128)(2,1)}, u32[]{:S(2)}, u32[]{:S(2)}) %collective-permute-start) | collective-permute-done | bytes 1179680 | tf_op jit(solution)/shard_map/ppermute | solution.py:10
  63.0 95.4 %collective-permute-start.2 = (bf16[512,1152]{1,0:T(8,128)(2,1)}, bf16[512,1152]{1,0:T(8,128)(2,1)}, u32[]{:S(2)}, u32[]{:S(2)}) collective-permute-start(bf16[512,1152]{1,0:T(8,128)(2,1)} %collective-permute-done), channel_id=1, source_target_pairs={{15,0},{0,1},{1,2},{2,3},{3,4},{4,5},{5,6},{6,7},{7,8},{8,9},{9,10... | collective-permute-start | bytes 3538952 | tf_op jit(solution)/shard_map/ppermute | solution.py:10
  158.3 3.6 fusion.29
  161.9 2.8 fusion.24
  164.7 1.1 convolution_convert_fusion.1
  165.8 3.4 collective-permute-start.4
  169.1 0.0 collective-permute-done.1
  169.2 2.8 fusion.25
  171.9 76.4 %collective-permute-done.2 = bf16[512,1152]{1,0:T(8,128)(2,1)} collective-permute-done((bf16[512,1152]{1,0:T(8,128)(2,1)}, bf16[512,1152]{1,0:T(8,128)(2,1)}, u32[]{:S(2)}, u32[]{:S(2)}) %collective-permute-start.2) | collective-permute-done | bytes 1179680 | tf_op jit(solution)/shard_map/ppermute | solution.py:10
  248.3 2.8 fusion.26
  251.1 1.1 convolution_convert_fusion
  252.2 1.9 collective-permute-start.5
  254.1 0.0 copy-start.2
  254.1 1.1 convolution_convert_fusion.2
  255.2 2.1 collective-permute-start.3
  257.3 0.0 copy-done.2
  257.3 2.2 convolution_add_fusion.2
  259.6 2.2 convolution_add_fusion.1
  261.8 19.7 %collective-permute-done.5 = bf16[512,1152]{1,0:T(8,128)(2,1)S(1)} collective-permute-done((bf16[512,1152]{1,0:T(8,128)(2,1)S(1)}, bf16[512,1152]{1,0:T(8,128)(2,1)S(1)}, u32[]{:S(2)}, u32[]{:S(2)}) %collective-permute-start.5) | collective-permute-done | bytes 1179680 | tf_op jit(solution)/shard_map/ppermute | solution.py:10
  281.4 1.9 collective-permute-start.6
  283.4 0.6 add_multiply_fusion
  283.9 2.5 fusion.6
  286.5 0.0 copy-start.3
  286.5 1.5 fusion.9
  288.0 7.1 %collective-permute-done.4 = bf16[512,1152]{1,0:T(8,128)(2,1)S(1)} collective-permute-done((bf16[512,1152]{1,0:T(8,128)(2,1)S(1)}, bf16[512,1152]{1,0:T(8,128)(2,1)S(1)}, u32[]{:S(2)}, u32[]{:S(2)}) %collective-permute-start.4) | collective-permute-done | bytes 1179680 | tf_op jit(solution)/shard_map/ppermute | solution.py:10
  295.1 76.4 %collective-permute-done.3 = bf16[512,1152]{1,0:T(8,128)(2,1)S(1)} collective-permute-done((bf16[512,1152]{1,0:T(8,128)(2,1)S(1)}, bf16[512,1152]{1,0:T(8,128)(2,1)S(1)}, u32[]{:S(2)}, u32[]{:S(2)}) %collective-permute-start.3) | collective-permute-done | bytes 1179680 | tf_op jit(solution)/shard_map/ppermute | solution.py:10
  371.6 32.6 %collective-permute-done.6 = bf16[512,1152]{1,0:T(8,128)(2,1)S(1)} collective-permute-done((bf16[512,1152]{1,0:T(8,128)(2,1)S(1)}, bf16[512,1152]{1,0:T(8,128)(2,1)S(1)}, u32[]{:S(2)}, u32[]{:S(2)}) %collective-permute-start.6) | collective-permute-done | bytes 1179680 | tf_op jit(solution)/shard_map/ppermute | solution.py:10
  404.2 0.0 copy-done.3
  404.2 1.5 fusion.11
  405.6 1.9 fusion.14
  (2 shorter events, 0.0 us)
Async XLA Ops:
  0.6 1.7 copy-start
  2.3 20.7 %copy-start.1 = (bf16[512,1152]{1,0:T(8,128)(2,1)S(1)}, bf16[512,1152]{1,0:T(8,128)(2,1)}, u32[]{:S(2)}) copy-start(bf16[512,1152]{1,0:T(8,128)(2,1)} %param.4) | copy-start | bytes 3538948
  2.6 60.3 %collective-permute-start = (bf16[512,1152]{1,0:T(8,128)(2,1)S(1)}, bf16[512,1152]{1,0:T(8,128)(2,1)}, u32[]{:S(2)}, u32[]{:S(2)}) collective-permute-start(bf16[512,1152]{1,0:T(8,128)(2,1)S(1)} %fusion.2), channel_id=1, source_target_pairs={{496,0},{0,16},{16,32},{32,48},{48,64},{64,80},{80,96},{96,112},{1... | collective-permute-start | bytes 3538952 | tf_op jit(solution)/shard_map/ppermute | solution.py:10
  18.2 151.0 %collective-permute-start.1 = (bf16[512,1152]{1,0:T(8,128)(2,1)S(1)}, bf16[512,1152]{1,0:T(8,128)(2,1)}, u32[]{:S(2)}, u32[]{:S(2)}) collective-permute-start(bf16[512,1152]{1,0:T(8,128)(2,1)S(1)} %fusion.2), channel_id=1, source_target_pairs={{15,0},{0,1},{1,2},{2,3},{3,4},{4,5},{5,6},{6,7},{7,8},{8,9},{9,10... | collective-permute-start | bytes 3538952 | tf_op jit(solution)/shard_map/ppermute | solution.py:10
  63.0 185.3 %collective-permute-start.2 = (bf16[512,1152]{1,0:T(8,128)(2,1)}, bf16[512,1152]{1,0:T(8,128)(2,1)}, u32[]{:S(2)}, u32[]{:S(2)}) collective-permute-start(bf16[512,1152]{1,0:T(8,128)(2,1)} %collective-permute-done), channel_id=1, source_target_pairs={{15,0},{0,1},{1,2},{2,3},{3,4},{4,5},{5,6},{6,7},{7,8},{8,9},{9,10... | collective-permute-start | bytes 3538952 | tf_op jit(solution)/shard_map/ppermute | solution.py:10
  165.8 129.3 %collective-permute-start.4 = (bf16[512,1152]{1,0:T(8,128)(2,1)S(1)}, bf16[512,1152]{1,0:T(8,128)(2,1)S(1)}, u32[]{:S(2)}, u32[]{:S(2)}) collective-permute-start(bf16[512,1152]{1,0:T(8,128)(2,1)S(1)} %convolution_convert_fusion.1), channel_id=1, source_target_pairs={{16,0},{32,16},{48,32},{64,48},{80,64},{96,80},{112,96},{128,112},... | collective-permute-start | bytes 3538952 | tf_op jit(solution)/shard_map/ppermute | solution.py:10
  252.2 29.3 %collective-permute-start.5 = (bf16[512,1152]{1,0:T(8,128)(2,1)S(1)}, bf16[512,1152]{1,0:T(8,128)(2,1)S(1)}, u32[]{:S(2)}, u32[]{:S(2)}) collective-permute-start(bf16[512,1152]{1,0:T(8,128)(2,1)S(1)} %convolution_convert_fusion), channel_id=1, source_target_pairs={{1,0},{2,1},{3,2},{4,3},{5,4},{6,5},{7,6},{8,7},{9,8},{10,9},{11,1... | collective-permute-start | bytes 3538952 | tf_op jit(solution)/shard_map/ppermute | solution.py:10
  254.1 3.2 copy-start.2
  255.2 116.3 %collective-permute-start.3 = (bf16[512,1152]{1,0:T(8,128)(2,1)S(1)}, bf16[512,1152]{1,0:T(8,128)(2,1)S(1)}, u32[]{:S(2)}, u32[]{:S(2)}) collective-permute-start(bf16[512,1152]{1,0:T(8,128)(2,1)S(1)} %convolution_convert_fusion.2), channel_id=1, source_target_pairs={{1,0},{2,1},{3,2},{4,3},{5,4},{6,5},{7,6},{8,7},{9,8},{10,9},{11,1... | collective-permute-start | bytes 3538952 | tf_op jit(solution)/shard_map/ppermute | solution.py:10
  281.4 122.7 %collective-permute-start.6 = (bf16[512,1152]{1,0:T(8,128)(2,1)S(1)}, bf16[512,1152]{1,0:T(8,128)(2,1)S(1)}, u32[]{:S(2)}, u32[]{:S(2)}) collective-permute-start(bf16[512,1152]{1,0:T(8,128)(2,1)S(1)} %collective-permute-done.5), channel_id=1, source_target_pairs={{16,0},{32,16},{48,32},{64,48},{80,64},{96,80},{112,96},{128,112},... | collective-permute-start | bytes 3538952 | tf_op jit(solution)/shard_map/ppermute | solution.py:10
  286.5 117.7 %copy-start.3 = (f32[512,512]{0,1:T(8,128)S(1)}, f32[512,512]{0,1:T(8,128)}, u32[]{:S(2)}) copy-start(f32[512,512]{0,1:T(8,128)} %get-tuple-element.8) | copy-start | bytes 3145732
where the time goes:
time: 408 us
  waiting for transfers between devices  249 us (61%)
  starting transfers between devices  124 us (30%)
  matrix products  26.1 us (6%)
  other arithmetic  6.26 us (2%)
    ppermute x7, waiting for transfers between devices, passed_along(): return lax.ppermute(block, axis, route)  249 us
    ppermute x7, starting transfers between devices, passed_along(): return lax.ppermute(block, axis, route)  124 us
    dot_general x4, matrix products, couple_weight(): jnp.dot(picture_tile_entries, caption_tile_entries.T, preferred_element_t...  10.8 us
    dot_general x4, matrix products, body(): jnp.dot(objective_weight, covered_couples, preferred_element_type=jnp.flo...  10.5 us
  transfers between devices with their start and end apart: 7, of which 6 were waited for; matrix products, arithmetic and copies ran while one was open for 7% of the time, Pallas kernels for 0%

commit v1 on v0

v1 whole, which is shorter than its diff:
```python
import jax
import jax.numpy as jnp
from jax import lax
from jax.experimental import pallas as pl
from jax.experimental.pallas import tpu as pltpu
from jax.sharding import PartitionSpec as P

MESH = pl.DeviceIdType.MESH
F32 = jnp.float32
BF16 = jnp.bfloat16

TXT, IMG = 0, 1
HOPS = 8
CHUNKS = 4
FIN_ROWS = 64

X_AT = 2 * HOPS
OWN_AT = X_AT + 4
N_SLOTS = OWN_AT + 2


def kernel(
    n_gx,
    n_gy,
    img_ref,
    txt_ref,
    scale_ref,
    offset_ref,
    loss_ref,
    img_out,
    txt_out,
    buf,
    own_n,
    acc,
    loss_acc,
    stage,
    ring_send,
    ring_recv,
    x_send,
    x_recv,
    local_sem,
    out_sem,
):
    rows_here, width = img_ref.shape
    part = rows_here // CHUNKS
    p, q = lax.axis_index("gx"), lax.axis_index("gy")
    core = lax.rem(q, 2)
    last = n_gy - 1

    def gx(value):
        return lax.rem(value + n_gx, n_gx)

    def device(gx_index, gy_index):
        return (gx_index, gy_index)

    wraps_up = q >= n_gy - 2
    wraps_down = q < 2
    up = device(jnp.where(wraps_up, gx(p + 1), p), jnp.where(wraps_up, core, q + 2))
    down = device(jnp.where(wraps_down, gx(p - 1), p), jnp.where(wraps_down, n_gy - 2 + core, q - 2))
    sibling = device(p, q + 1 - 2 * core)
    ninth_to = device(
        jnp.where(core == 1, jnp.where(q == last, gx(p - 1), p), jnp.where(q == 0, gx(p + 1), p)),
        jnp.where(core == 1, jnp.where(q == last, 0, q + 1), jnp.where(q == 0, last, q - 1)),
    )
    ninth_from = device(
        jnp.where(core == 0, jnp.where(q == 0, gx(p + 1), p), jnp.where(q == last, gx(p - 1), p)),
        jnp.where(core == 0, jnp.where(q == 0, last, q - 1), jnp.where(q == last, 0, q + 1)),
    )

    barrier = pltpu.get_barrier_semaphore()
    for source in (up, down, sibling, ninth_from):
        pl.semaphore_signal(barrier, inc=1, device_id=source, device_id_type=MESH)
    pl.semaphore_wait(barrier, 4)

    def piece(j):
        return pl.ds(pl.multiple_of(j * part, part), part)

    def ring_copy(kind, hop, j, src):
        return pltpu.make_async_remote_copy(
            src_ref=src,
            dst_ref=buf.at[kind * HOPS + hop - 1, piece(j)],
            send_sem=ring_send.at[kind, hop - 1, j],
            recv_sem=ring_recv.at[kind, hop - 1, j],
            device_id=up if kind == TXT else down,
            device_id_type=MESH,
        )

    def x_copy(slot, j, src, target):
        return pltpu.make_async_remote_copy(
            src_ref=src,
            dst_ref=buf.at[X_AT + slot, piece(j)],
            send_sem=x_send.at[slot, j],
            recv_sem=x_recv.at[slot, j],
            device_id=target,
            device_id_type=MESH,
        )

    def ring_at(kind, hop, j):
        return buf.at[kind * HOPS + hop - 1, piece(j)]

    inputs = (txt_ref, img_ref)
    short = core
    for j in range(CHUNKS):
        for kind in (TXT, IMG):
            ring_copy(kind, 1, j, inputs[kind].at[piece(j)]).start()
    own_loads = [
        pltpu.make_async_copy(inputs[kind], buf.at[OWN_AT + kind], local_sem.at[kind])
        for kind in (TXT, IMG)
    ]
    for load in own_loads:
        load.start()
    for j in range(CHUNKS):
        for kind in (TXT, IMG):

            @pl.when(short == kind)
            def _():
                x_copy(0, j, inputs[kind].at[piece(j)], sibling).start()

    scale, offset = scale_ref[0], offset_ref[0]
    acc[...] = jnp.zeros_like(acc)
    loss_acc[...] = jnp.zeros_like(loss_acc)
    for load in own_loads:
        load.wait()

    def unit(raw):
        wide = raw.astype(F32)
        inverse = lax.rsqrt(jnp.sum(wide * wide, axis=-1, keepdims=True) + 1e-06)
        return wide * inverse, inverse

    for kind in (TXT, IMG):

        def normalize_own(i, _):
            at = pl.ds(pl.multiple_of(i * FIN_ROWS, FIN_ROWS), FIN_ROWS)
            own_n[kind, at] = unit(buf[OWN_AT + kind, at])[0].astype(BF16)
            return 0

        lax.fori_loop(0, rows_here // FIN_ROWS, normalize_own, 0)

    def visit(slot, j, kind, own_pair):
        block = unit(buf[slot, piece(j)])[0].astype(BF16)
        scores = lax.dot_general(
            own_n[1 - kind], block, (((1,), (1,)), ((), ())), preferred_element_type=F32
        )
        logits = scale * scores + offset
        same = lax.broadcasted_iota(jnp.int32, logits.shape, 0) == (
            lax.broadcasted_iota(jnp.int32, logits.shape, 1) + j * part
        )
        match = jnp.logical_and(same, own_pair)
        drive = jnp.where(match, -logits, logits)
        small = jnp.exp(-jnp.abs(drive))
        whole = 1.0 / (1.0 + small)
        sigmoid = jnp.where(drive >= 0, whole, small * whole)
        coef = (jnp.where(match, -scale, scale) * sigmoid).astype(BF16)

        @pl.when(kind == TXT)
        def _():
            loss_acc[...] += jnp.maximum(drive, 0.0) + jnp.log1p(small)

        acc[kind] += jnp.dot(coef, block, preferred_element_type=F32)

    def finish(kind):
        def some_rows(i, _):
            at = pl.ds(pl.multiple_of(i * FIN_ROWS, FIN_ROWS), FIN_ROWS)
            direction = acc[kind, at]
            u, inverse = unit(buf[OWN_AT + 1 - kind, at])
            grad = inverse * (direction - u * jnp.sum(u * direction, axis=-1, keepdims=True))
            stage[kind, at] = grad.astype(BF16)
            return 0

        lax.fori_loop(0, rows_here // FIN_ROWS, some_rows, 0)
        for one, out in ((TXT, img_out), (IMG, txt_out)):

            @pl.when(kind == one)
            def _():
                pltpu.make_async_copy(stage.at[one], out, out_sem.at[one]).start()

    def step(s, _):
        def chunk(j, _):
            @pl.when(jnp.logical_and(s >= 1, s <= HOPS))
            def _():
                for kind in (TXT, IMG):
                    ring_copy(kind, s, j, ring_at(kind, s, j)).wait_recv()

                    @pl.when(s < HOPS)
                    def _():
                        ring_copy(kind, s + 1, j, ring_at(kind, s, j)).start()

                    @pl.when(jnp.logical_and(s == HOPS, short != kind))
                    def _():
                        x_copy(3, j, ring_at(kind, s, j), ninth_to).start()

                    @pl.when(jnp.logical_and(s == HOPS, short == kind))
                    def _():
                        x_copy(1, j, ring_at(kind, s, j), sibling).start()

                    @pl.when(jnp.logical_and(s == 1, short != kind))
                    def _():
                        x_copy(2, j, ring_at(kind, s, j), sibling).start()

            @pl.when(jnp.logical_and(s == HOPS + 1, j == 0))
            def _():
                finish(1 - core)

            n_visits = jnp.where(
                s == 0, 2, jnp.where(s == HOPS, 3, jnp.where(jnp.logical_or(s <= 2, s > HOPS), 1, 0))
            )

            def one(v, _):
                from_x = jnp.logical_or(jnp.logical_and(s >= 1, s != HOPS), v == 2)
                x_slot = jnp.where(s == 1, 0, jnp.where(s == 2, 2, jnp.where(s == HOPS, 1, 3)))

                @pl.when(from_x)
                def _():
                    x_copy(x_slot, j, buf.at[X_AT, piece(j)], sibling).wait_recv()

                slot = jnp.where(
                    s == 0, OWN_AT + v, jnp.where(from_x, X_AT + x_slot, v * HOPS + HOPS - 1)
                )
                x_kind = jnp.where(jnp.logical_or(s == 1, s == HOPS), 1 - core, core)
                visit(slot, j, jnp.where(from_x, x_kind, v), s == 0)
                return 0

            lax.fori_loop(0, n_visits, one, 0)
            return 0

        lax.fori_loop(0, CHUNKS, chunk, 0)
        return 0

    lax.fori_loop(0, HOPS + 2, step, 0)
    finish(core)
    loss_ref[...] = jnp.sum(loss_acc[...].T, axis=0, keepdims=True) / (4.0 * rows_here)

    def drain(j, _):
        def hop(s, _):
            for kind in (TXT, IMG):
                ring_copy(kind, s, j, ring_at(kind, s, j)).wait_send()
            return 0

        lax.fori_loop(1, HOPS + 1, hop, 0)
        for slot in range(4):
            x_copy(slot, j, buf.at[X_AT, piece(j)], sibling).wait_send()
        return 0

    lax.fori_loop(0, CHUNKS, drain, 0)
    for one, out in ((TXT, img_out), (IMG, txt_out)):
        pltpu.make_async_copy(stage.at[one], out, out_sem.at[one]).wait()


def solution(mesh):
    n_gx, n_gy = mesh.shape["gx"], mesh.shape["gy"]

    def body(img, txt, scale, offset):
        rows, width = img.shape
        part = rows // CHUNKS

        def run(*refs):
            kernel(n_gx, n_gy, *refs)

        any_space = pl.BlockSpec(memory_space=pl.ANY)
        smem = pl.BlockSpec(memory_space=pltpu.SMEM)
        loss, img_grad, txt_grad = pl.pallas_call(
            run,
            out_shape=(
                jax.ShapeDtypeStruct((1, rows), F32),
                jax.ShapeDtypeStruct((rows, width), BF16),
                jax.ShapeDtypeStruct((rows, width), BF16),
            ),
            in_specs=[any_space, any_space, smem, smem],
            out_specs=(pl.BlockSpec(memory_space=pltpu.VMEM), any_space, any_space),
            scratch_shapes=[
                pltpu.VMEM((N_SLOTS, rows, width), BF16),
                pltpu.VMEM((2, rows, width), BF16),
                pltpu.VMEM((2, rows, width), F32),
                pltpu.VMEM((rows, part), F32),
                pltpu.VMEM((2, rows, width), BF16),
                pltpu.SemaphoreType.DMA((2, HOPS, CHUNKS)),
                pltpu.SemaphoreType.DMA((2, HOPS, CHUNKS)),
                pltpu.SemaphoreType.DMA((4, CHUNKS)),
                pltpu.SemaphoreType.DMA((4, CHUNKS)),
                pltpu.SemaphoreType.DMA((2,)),
                pltpu.SemaphoreType.DMA((2,)),
            ],
            compiler_params=pltpu.CompilerParams(
                collective_id=0, has_side_effects=True, vmem_limit_bytes=56 * 1024 * 1024
            ),
            cost_estimate=pl.CostEstimate(
                flops=14 * 2 * rows * rows * width, bytes_accessed=8 * rows * width, transcendentals=0
            ),
        )(img, txt, scale, offset)
        return loss.reshape(rows), img_grad, txt_grad

    return jax.shard_map(
        body,
        mesh=mesh,
        in_specs=(P(("gx", "gy"), None), P(("gx", "gy"), None), P(), P()),
        out_specs=(P(("gx", "gy")), P(("gx", "gy"), None), P(("gx", "gy"), None)),
        check_vma=False,
    )
```

time: 408 us -> 244 us (0.60)
  the two profiles are of different devices: /device:TPU:7 before, /device:TPU:1 now
where the time goes in v1:
time: 244 us
  Pallas kernels  237 us (97%)
  local copies, waits for them, and re-layouts  4.74 us (2%)
    pallas_call x1, Pallas kernels, body(): pl.pallas_call(run, out_shape=(jax.ShapeDtypeStruct((1, rows), F32), jax....  237 us

profile of v1, /device:TPU:1, one launch (start us, length us, event | category | flops | bytes accessed | tf_op | source)
XLA Modules:
  0.0 243.6 jit_solution(17766239135469618209)
XLA Ops:
  1.9 236.9 %shard_map.67 = (f32[1,512]{1,0:T(1,128)}, bf16[512,1152]{1,0:T(8,128)(2,1)}, bf16[512,1152]{1,0:T(8,128)(2,1)}) custom-call(bf16[512,1152]{1,0:T(8,128)(2,1)} %refs_0_.1, bf16[512,1152]{1,0:T(8,128)(2,1)} %refs_1_.1, f32[1]{0:T(128)S(6)} %copy.10.refs_2_, f32[1]{0:T(128)S(6)} %copy.11.refs_3_), custom_call_target="tpu_custom_call" | custom-call | flops 8455716864 | bytes 4718592 | tf_op jit(solution)/shard_map/pallas_call | solution.py:261
  238.9 1.3 copy.12
  240.1 0.0 copy-start
  240.1 2.5 %copy.13 = bf16[512,1152]{1,0:T(8,128)(2,1)} copy(bf16[512,1152]{1,0:T(8,128)(2,1)} %get-tuple-element.13) | data formatting | bytes 2359296
  242.6 0.0 copy-done
  242.6 1.0 copy.14
Async XLA Ops:
  240.1 2.5 %copy-start = (bf16[512,1152]{1,0:T(8,128)(2,1)S(1)}, bf16[512,1152]{1,0:T(8,128)(2,1)}, u32[]{:S(2)}) copy-start(bf16[512,1152]{1,0:T(8,128)(2,1)} %get-tuple-element.14) | copy-start | bytes 3538948

commit v2 on v1

--- a/solution.py
+++ b/solution.py
@@ -12,6 +12,7 @@
 TXT, IMG = 0, 1
 HOPS = 8
 CHUNKS = 4
+IN_FLIGHT = 2
 FIN_ROWS = 64
 
 X_AT = 2 * HOPS
@@ -26,20 +27,17 @@
     txt_ref,
     scale_ref,
     offset_ref,
+    grads_ref,
     loss_ref,
-    img_out,
-    txt_out,
     buf,
     own_n,
     acc,
     loss_acc,
-    stage,
     ring_send,
     ring_recv,
     x_send,
     x_recv,
     local_sem,
-    out_sem,
 ):
     rows_here, width = img_ref.shape
     part = rows_here // CHUNKS
@@ -100,22 +98,14 @@
 
     inputs = (txt_ref, img_ref)
     short = core
-    for j in range(CHUNKS):
-        for kind in (TXT, IMG):
-            ring_copy(kind, 1, j, inputs[kind].at[piece(j)]).start()
+    for kind in (TXT, IMG):
+        ring_copy(kind, 1, 0, inputs[kind].at[piece(0)]).start()
     own_loads = [
         pltpu.make_async_copy(inputs[kind], buf.at[OWN_AT + kind], local_sem.at[kind])
         for kind in (TXT, IMG)
     ]
     for load in own_loads:
         load.start()
-    for j in range(CHUNKS):
-        for kind in (TXT, IMG):
-
-            @pl.when(short == kind)
-            def _():
-                x_copy(0, j, inputs[kind].at[piece(j)], sibling).start()
-
     scale, offset = scale_ref[0], offset_ref[0]
     acc[...] = jnp.zeros_like(acc)
     loss_acc[...] = jnp.zeros_like(loss_acc)
@@ -164,86 +154,116 @@
             direction = acc[kind, at]
             u, inverse = unit(buf[OWN_AT + 1 - kind, at])
             grad = inverse * (direction - u * jnp.sum(u * direction, axis=-1, keepdims=True))
-            stage[kind, at] = grad.astype(BF16)
+            grads_ref[kind, at] = grad.astype(BF16)
             return 0
 
         lax.fori_loop(0, rows_here // FIN_ROWS, some_rows, 0)
-        for one, out in ((TXT, img_out), (IMG, txt_out)):
-
-            @pl.when(kind == one)
-            def _():
-                pltpu.make_async_copy(stage.at[one], out, out_sem.at[one]).start()
-
-    def step(s, _):
-        def chunk(j, _):
-            @pl.when(jnp.logical_and(s >= 1, s <= HOPS))
-            def _():
-                for kind in (TXT, IMG):
-                    ring_copy(kind, s, j, ring_at(kind, s, j)).wait_recv()
-
-                    @pl.when(s < HOPS)
-                    def _():
-                        ring_copy(kind, s + 1, j, ring_at(kind, s, j)).start()
-
-                    @pl.when(jnp.logical_and(s == HOPS, short != kind))
-                    def _():
-                        x_copy(3, j, ring_at(kind, s, j), ninth_to).start()
-
-                    @pl.when(jnp.logical_and(s == HOPS, short == kind))
-                    def _():
-                        x_copy(1, j, ring_at(kind, s, j), sibling).start()
-
-                    @pl.when(jnp.logical_and(s == 1, short != kind))
-                    def _():
-                        x_copy(2, j, ring_at(kind, s, j), sibling).start()
-
-            @pl.when(jnp.logical_and(s == HOPS + 1, j == 0))
-            def _():
-                finish(1 - core)
-
-            n_visits = jnp.where(
-                s == 0, 2, jnp.where(s == HOPS, 3, jnp.where(jnp.logical_or(s <= 2, s > HOPS), 1, 0))
+
+    sends = HOPS * CHUNKS
+    tail = sends - 2
+    extra = sends + CHUNKS
+
+    def within(i, low, count):
+        return jnp.logical_and(i >= low, i < low + count)
+
+    def turn(i, _):
+        s, j = lax.div(i, CHUNKS), lax.rem(i, CHUNKS)
+        before = jnp.maximum(i - IN_FLIGHT, 0)
+        for kind in (TXT, IMG):
+
+            @pl.when(within(i, IN_FLIGHT, sends))
+            def _():
+                at = lax.rem(before, CHUNKS)
+                ring_copy(kind, lax.div(before, CHUNKS) + 1, at, ring_at(kind, 1, at)).wait_send()
+
+            @pl.when(jnp.logical_and(within(i, sends + IN_FLIGHT, CHUNKS), short != kind))
+            def _():
+                at = lax.rem(before, CHUNKS)
+                x_copy(3, at, ring_at(kind, HOPS, at), ninth_to).wait_send()
+
+            @pl.when(within(i, 1, CHUNKS - 1))
+            def _():
+                ring_copy(kind, 1, j, inputs[kind].at[piece(j)]).start()
+
+            @pl.when(within(i, CHUNKS, sends - CHUNKS))
+            def _():
+                ring_copy(kind, s, j, ring_at(kind, s, j)).wait_recv()
+                ring_copy(kind, s + 1, j, ring_at(kind, s, j)).start()
+
+            @pl.when(jnp.logical_and(within(i, sends, CHUNKS), short != kind))
+            def _():
+                x_copy(3, j, ring_at(kind, HOPS, j), ninth_to).start()
+
+            @pl.when(jnp.logical_and(within(i, 0, CHUNKS), short == kind))
+            def _():
+                x_copy(0, j, inputs[kind].at[piece(j)], sibling).start()
+
+            @pl.when(jnp.logical_and(within(i, CHUNKS, CHUNKS), short != kind))
+            def _():
+                x_copy(2, j, ring_at(kind, 1, j), sibling).start()
+
+            @pl.when(within(i, tail, CHUNKS))
+            def _():
+                at = i - tail
+                ring_copy(kind, HOPS, at, ring_at(kind, HOPS, at)).wait_recv()
+
+                @pl.when(short == kind)
+                def _():
+                    x_copy(1, at, ring_at(kind, HOPS, at), sibling).start()
+
+        @pl.when(i == extra)
+        def _():
+            finish(1 - core)
+
+        in_tail = within(i, tail, CHUNKS)
+        pairs = jnp.where(jnp.logical_or(i < CHUNKS, in_tail), 2, 0)
+        x_early = within(i, CHUNKS, 2 * CHUNKS)
+        x_tail = within(i, tail + 1, CHUNKS)
+        x_last = i >= extra
+        from_x = jnp.where(jnp.logical_or(jnp.logical_or(x_early, x_tail), x_last), 1, 0)
+        x_slot = jnp.where(x_last, 3, jnp.where(x_tail, 1, jnp.where(s == 1, 0, 2)))
+        x_piece = jnp.where(x_tail, i - tail - 1, j)
+        x_kind = jnp.where(x_slot < 2, 1 - core, core)
+
+        def one(v, _):
+            is_x = v >= pairs
+
+            @pl.when(is_x)
+            def _():
+                x_copy(x_slot, x_piece, buf.at[X_AT, piece(x_piece)], sibling).wait_recv()
+
+            slot = jnp.where(
+                is_x, X_AT + x_slot, jnp.where(in_tail, v * HOPS + HOPS - 1, OWN_AT + v)
             )
-
-            def one(v, _):
-                from_x = jnp.logical_or(jnp.logical_and(s >= 1, s != HOPS), v == 2)
-                x_slot = jnp.where(s == 1, 0, jnp.where(s == 2, 2, jnp.where(s == HOPS, 1, 3)))
-
-                @pl.when(from_x)
-                def _():
-                    x_copy(x_slot, j, buf.at[X_AT, piece(j)], sibling).wait_recv()
-
-                slot = jnp.where(
-                    s == 0, OWN_AT + v, jnp.where(from_x, X_AT + x_slot, v * HOPS + HOPS - 1)
-                )
-                x_kind = jnp.where(jnp.logical_or(s == 1, s == HOPS), 1 - core, core)
-                visit(slot, j, jnp.where(from_x, x_kind, v), s == 0)
-                return 0
-
-            lax.fori_loop(0, n_visits, one, 0)
+            at = jnp.where(is_x, x_piece, jnp.where(in_tail, i - tail, j))
+            visit(slot, at, jnp.where(is_x, x_kind, v), i < CHUNKS)
             return 0
 
-        lax.fori_loop(0, CHUNKS, chunk, 0)
+        lax.fori_loop(0, pairs + from_x, one, 0)
         return 0
 
-    lax.fori_loop(0, HOPS + 2, step, 0)
+    lax.fori_loop(0, extra + CHUNKS, turn, 0)
     finish(core)
     loss_ref[...] = jnp.sum(loss_acc[...].T, axis=0, keepdims=True) / (4.0 * rows_here)
 
     def drain(j, _):
-        def hop(s, _):
-            for kind in (TXT, IMG):
-                ring_copy(kind, s, j, ring_at(kind, s, j)).wait_send()
-            return 0
-
-        lax.fori_loop(1, HOPS + 1, hop, 0)
-        for slot in range(4):
+        for slot in range(3):
             x_copy(slot, j, buf.at[X_AT, piece(j)], sibling).wait_send()
         return 0
 
     lax.fori_loop(0, CHUNKS, drain, 0)
-    for one, out in ((TXT, img_out), (IMG, txt_out)):
-        pltpu.make_async_copy(stage.at[one], out, out_sem.at[one]).wait()
+
+
+def hand_out(grads_ref, loss_in, img_out, txt_out, loss_out, sems):
+    copies = [
+        pltpu.make_async_copy(grads_ref.at[one], out, sems.at[one])
+        for one, out in ((TXT, img_out), (IMG, txt_out))
+    ]
+    for copy in copies:
+        copy.start()
+    loss_out[...] = loss_in[...]
+    for copy in copies:
+        copy.wait()
 
 
 def solution(mesh):
@@ -258,35 +278,41 @@
 
         any_space = pl.BlockSpec(memory_space=pl.ANY)
         smem = pl.BlockSpec(memory_space=pltpu.SMEM)
-        loss, img_grad, txt_grad = pl.pallas_call(
+        vmem = pl.BlockSpec(memory_space=pltpu.VMEM)
+        grads, loss = pl.pallas_call(
             run,
-            out_shape=(
-                jax.ShapeDtypeStruct((1, rows), F32),
-                jax.ShapeDtypeStruct((rows, width), BF16),
-                jax.ShapeDtypeStruct((rows, width), BF16),
-            ),
+            out_shape=(pltpu.VMEM((2, rows, width), BF16), pltpu.VMEM((1, rows), F32)),
             in_specs=[any_space, any_space, smem, smem],
-            out_specs=(pl.BlockSpec(memory_space=pltpu.VMEM), any_space, any_space),
+            out_specs=(vmem, vmem),
             scratch_shapes=[
                 pltpu.VMEM((N_SLOTS, rows, width), BF16),
                 pltpu.VMEM((2, rows, width), BF16),
                 pltpu.VMEM((2, rows, width), F32),
                 pltpu.VMEM((rows, part), F32),
-                pltpu.VMEM((2, rows, width), BF16),
                 pltpu.SemaphoreType.DMA((2, HOPS, CHUNKS)),
                 pltpu.SemaphoreType.DMA((2, HOPS, CHUNKS)),
                 pltpu.SemaphoreType.DMA((4, CHUNKS)),
                 pltpu.SemaphoreType.DMA((4, CHUNKS)),
                 pltpu.SemaphoreType.DMA((2,)),
-                pltpu.SemaphoreType.DMA((2,)),
             ],
             compiler_params=pltpu.CompilerParams(
-                collective_id=0, has_side_effects=True, vmem_limit_bytes=56 * 1024 * 1024
+                collective_id=0, has_side_effects=True, vmem_limit_bytes=52 * 1024 * 1024
             ),
             cost_estimate=pl.CostEstimate(
                 flops=14 * 2 * rows * rows * width, bytes_accessed=8 * rows * width, transcendentals=0
             ),
         )(img, txt, scale, offset)
+        img_grad, txt_grad, loss = pl.pallas_call(
+            hand_out,
+            out_shape=(
+                jax.ShapeDtypeStruct((rows, width), BF16),
+                jax.ShapeDtypeStruct((rows, width), BF16),
+                jax.ShapeDtypeStruct((1, rows), F32),
+            ),
+            in_specs=[vmem, vmem],
+            out_specs=(any_space, any_space, vmem),
+            scratch_shapes=[pltpu.SemaphoreType.DMA((2,))],
+        )(grads, loss)
         return loss.reshape(rows), img_grad, txt_grad
 
     return jax.shard_map(

time: 244 us -> 249 us (1.020)
  Pallas kernels: 237 us -> 244 us
  local copies, waits for them, and re-layouts: 4.74 us -> 2 us
    pallas_call x1 -> x2, Pallas kernels: 237 us -> 244 us  [the longest x1 240 us: body(): pl.pallas_call(run, out_shape=(pltpu.VMEM((2, rows, width), BF16), pltpu....]
    unnamed x5 -> x4, local copies, waits for them, and re-layouts: 4.74 us -> 2 us
where the time goes in v2:
time: 249 us; the launch traced here: 248 us
  Pallas kernels  244 us (98%)
    pallas_call x1, Pallas kernels, body(): pl.pallas_call(run, out_shape=(pltpu.VMEM((2, rows, width), BF16), pltpu....  240 us

profile of v2, /device:TPU:1, one launch (start us, length us, event | category | flops | bytes accessed | tf_op | source)
XLA Modules:
  0.0 247.8 jit_solution(2859801155926989520)
XLA Ops:
  1.9 240.2 %shard_map.67 = (bf16[2,512,1152]{2,1,0:T(8,128)(2,1)S(1)}, f32[1,512]{1,0:T(1,128)S(1)}) custom-call(bf16[512,1152]{1,0:T(8,128)(2,1)} %refs_0_.1, bf16[512,1152]{1,0:T(8,128)(2,1)} %refs_1_.1, f32[1]{0:T(128)S(6)} %copy.7.refs_2_, f32[1]{0:T(128)S(6)} %copy.8.refs_3_), custom_call_target="tpu_custom_call" | custom-call | flops 8455716864 | bytes 4718592 | tf_op jit(solution)/shard_map/pallas_call | solution.py:282
  242.1 0.0 copy-start
  242.1 1.4 copy-done
  243.5 0.0 copy-start.1
  243.5 0.6 copy-done.1
  244.1 3.7 %shard_map.68 = (bf16[512,1152]{1,0:T(8,128)(2,1)}, bf16[512,1152]{1,0:T(8,128)(2,1)}, f32[1,512]{1,0:T(1,128)}) custom-call(bf16[2,512,1152]{2,1,0:T(8,128)(2,1)} %copy-done, f32[1,512]{1,0:T(1,128)} %copy-done.1), custom_call_target="tpu_custom_call" | custom-call | tf_op jit(solution)/shard_map/pallas_call | solution.py:305
Async XLA Ops:
  242.1 1.4 copy-start
  243.5 0.6 copy-start.1

commit v3 on v2

v3 whole, which is shorter than its diff:
```python
import jax
import jax.numpy as jnp
from jax import lax
from jax.experimental import pallas as pl
from jax.experimental.pallas import tpu as pltpu
from jax.sharding import PartitionSpec as P

MESH = pl.DeviceIdType.MESH
F32 = jnp.float32
BF16 = jnp.bfloat16

TXT, IMG = 0, 1
HOPS = 8
PIECES = 4
HALVES = 2
SEMS = 16
SUB = 64
FIN_ROWS = 32

X_AT = 2 * HOPS
OWN_AT = X_AT + 4
N_SLOTS = OWN_AT + 2


def kernel(
    n_gx,
    n_gy,
    img_ref,
    txt_ref,
    scale_ref,
    offset_ref,
    grads_ref,
    loss_ref,
    buf,
    own_n,
    acc,
    loss_acc,
    block,
    scores,
    coef,
    ring_send,
    ring_recv,
    x_send,
    x_recv,
    local_sem,
):
    rows_here, width = img_ref.shape
    part, half = rows_here // PIECES, rows_here // HALVES
    sends = HOPS * PIECES
    p, q = lax.axis_index("gx"), lax.axis_index("gy")
    core = lax.rem(q, 2)
    last = n_gy - 1

    def gx(value):
        return lax.rem(value + n_gx, n_gx)

    def device(gx_index, gy_index):
        return (gx_index, gy_index)

    wraps_up = q >= n_gy - 2
    wraps_down = q < 2
    up = device(jnp.where(wraps_up, gx(p + 1), p), jnp.where(wraps_up, core, q + 2))
    down = device(jnp.where(wraps_down, gx(p - 1), p), jnp.where(wraps_down, n_gy - 2 + core, q - 2))
    sibling = device(p, q + 1 - 2 * core)
    ninth_to = device(
        jnp.where(core == 1, jnp.where(q == last, gx(p - 1), p), jnp.where(q == 0, gx(p + 1), p)),
        jnp.where(core == 1, jnp.where(q == last, 0, q + 1), jnp.where(q == 0, last, q - 1)),
    )
    ninth_from = device(
        jnp.where(core == 0, jnp.where(q == 0, gx(p + 1), p), jnp.where(q == last, gx(p - 1), p)),
        jnp.where(core == 0, jnp.where(q == 0, last, q - 1), jnp.where(q == last, 0, q + 1)),
    )

    barrier = pltpu.get_barrier_semaphore()
    for source in (up, down, sibling, ninth_from):
        pl.semaphore_signal(barrier, inc=1, device_id=source, device_id_type=MESH)
    pl.semaphore_wait(barrier, 4)

    def piece(j):
        return pl.ds(pl.multiple_of(j * part, part), part)

    def half_of(h):
        return pl.ds(pl.multiple_of(h * half, half), half)

    def landing(kind, n):
        return buf.at[kind * HOPS + lax.div(n, PIECES), piece(lax.rem(n, PIECES))]

    def ring_copy(kind, n, src):
        return pltpu.make_async_remote_copy(
            src_ref=src,
            dst_ref=landing(kind, n),
            send_sem=ring_send.at[kind, lax.rem(n, SEMS)],
            recv_sem=ring_recv.at[kind, n],
            device_id=up if kind == TXT else down,
            device_id_type=MESH,
        )

    def x_copy(slot, j, src, target):
        return pltpu.make_async_remote_copy(
            src_ref=src,
            dst_ref=buf.at[X_AT + slot, piece(j)],
            send_sem=x_send.at[slot, j],
            recv_sem=x_recv.at[slot, j],
            device_id=target,
            device_id_type=MESH,
        )

    inputs = (txt_ref, img_ref)
    short = core

    def set_out(n):
        n = jnp.int32(n)
        for kind in (TXT, IMG):
            ring_copy(kind, n, inputs[kind].at[piece(n)]).start()

    def unit(raw):
        wide = raw.astype(F32)
        return wide * lax.rsqrt(jnp.sum(wide * wide, axis=-1, keepdims=True) + 1e-06)

    def normalize_own(kind):
        def some_rows(i, _):
            at = pl.ds(pl.multiple_of(i * FIN_ROWS, FIN_ROWS), FIN_ROWS)
            own_n[kind, at] = unit(buf[OWN_AT + kind, at]).astype(BF16)
            return 0

        lax.fori_loop(0, rows_here // FIN_ROWS, some_rows, 0)

    set_out(0)
    own_loads = [
        pltpu.make_async_copy(inputs[kind], buf.at[OWN_AT + kind], local_sem.at[kind])
        for kind in (TXT, IMG)
    ]
    for load in own_loads:
        load.start()
    scale, offset = scale_ref[0], offset_ref[0]
    acc[...] = jnp.zeros_like(acc)
    loss_acc[...] = jnp.zeros_like(loss_acc)
    set_out(1)
    for load in own_loads:
        load.wait()
    normalize_own(TXT)
    set_out(2)
    normalize_own(IMG)
    set_out(3)

    def weigh(h, own_pair, with_loss):
        def some_rows(i, _):
            at = pl.ds(pl.multiple_of(i * SUB, SUB), SUB)
            drive = scale * scores[at] + offset
            weight = scale
            if own_pair:
                row = lax.broadcasted_iota(jnp.int32, drive.shape, 0) + i * SUB
                match = row == lax.broadcasted_iota(jnp.int32, drive.shape, 1) + h * half
                drive = jnp.where(match, -drive, drive)
                weight = jnp.where(match, -scale, scale)
            power = jnp.exp(drive)
            coef[at] = (weight * (power * (1.0 / (1.0 + power)))).astype(BF16)
            if with_loss:
                loss = jnp.log1p(power)
                fold = half // 2
                loss_acc[at] += loss[:, :fold] + loss[:, fold:]
            return 0

        lax.fori_loop(0, rows_here // SUB, some_rows, 0, unroll=2)

    def visit(slot, h, kind, own_pair):
        def some_rows(i, _):
            at = pl.ds(pl.multiple_of(h * half + i * FIN_ROWS, FIN_ROWS), FIN_ROWS)
            to = pl.ds(pl.multiple_of(i * FIN_ROWS, FIN_ROWS), FIN_ROWS)
            block[to] = unit(buf[slot, at]).astype(BF16)
            return 0

        lax.fori_loop(0, half // FIN_ROWS, some_rows, 0, unroll=4)
        for r in range(HALVES):
            at = pl.ds(r * half, half)
            scores[at] = lax.dot_general(
                own_n[1 - kind, at], block[...], (((1,), (1,)), ((), ())), preferred_element_type=F32
            )
        for one in (TXT, IMG):

            @pl.when(jnp.logical_and(own_pair, kind == one))
            def _():
                weigh(h, True, one == TXT)

            @pl.when(jnp.logical_and(jnp.logical_not(own_pair), kind == one))
            def _():
                weigh(h, False, one == TXT)

        for r in range(HALVES):
            at = pl.ds(r * half, half)
            acc[kind, at] += jnp.dot(coef[at], block[...], preferred_element_type=F32)

    def finish(kind):
        def some_rows(i, _):
            at = pl.ds(pl.multiple_of(i * FIN_ROWS, FIN_ROWS), FIN_ROWS)
            direction = acc[kind, at]
            raw = buf[OWN_AT + 1 - kind, at].astype(F32)
            inverse = lax.rsqrt(jnp.sum(raw * raw, axis=-1, keepdims=True) + 1e-06)
            along = jnp.sum(raw * direction, axis=-1, keepdims=True) * (inverse * inverse * inverse)
            grads_ref[kind, at] = (inverse * direction - along * raw).astype(BF16)
            return 0

        lax.fori_loop(0, rows_here // FIN_ROWS, some_rows, 0, unroll=4)

    def within(i, low, count):
        return jnp.logical_and(i >= low, i < low + count)

    ending = sends - 3

    def turn(i, _):
        t = jnp.where(i > ending, i - 1, i)

        @pl.when(jnp.logical_and(t < sends, i != ending + 1))
        def _():
            onward = t + PIECES
            j = lax.rem(t, PIECES)
            for kind in (TXT, IMG):
                ring_copy(kind, t, landing(kind, t)).wait_recv()

                @pl.when(onward < sends)
                def _():
                    ring_copy(kind, onward, landing(kind, t)).start()

                @pl.when(jnp.logical_and(onward >= sends, short != kind))
                def _():
                    x_copy(3, j, landing(kind, t), ninth_to).start()

                @pl.when(jnp.logical_and(onward >= sends, short == kind))
                def _():
                    x_copy(1, j, landing(kind, t), sibling).start()

                @pl.when(jnp.logical_and(t < PIECES, short != kind))
                def _():
                    x_copy(2, j, landing(kind, t), sibling).start()

                @pl.when(jnp.logical_and(t < PIECES, short == kind))
                def _():
                    x_copy(0, j, inputs[kind].at[piece(j)], sibling).start()

                @pl.when(t >= PIECES)
                def _():
                    ring_copy(kind, t - PIECES, landing(kind, t)).wait_send()

        since = i - ending

        @pl.when(since == 7)
        def _():
            finish(1 - core)

        is_end = since >= 0
        is_own = i < 4
        is_x_early = within(i, 4, 4)
        step = lax.rem(jnp.maximum(since, 0), 3)
        is_x3 = since >= 6
        is_x1 = jnp.logical_and(within(since, 0, 6), step == 2)
        is_x = jnp.logical_or(is_x_early, jnp.logical_or(is_x1, is_x3))
        x_slot = jnp.where(is_x3, 3, jnp.where(is_x1, 1, jnp.where(i < 6, 0, 2)))
        kind = jnp.where(
            is_x, jnp.where(x_slot < 2, 1 - core, core), jnp.where(is_end, step, lax.rem(i, 2))
        )
        slot = jnp.where(
            is_x, X_AT + x_slot, jnp.where(is_end, kind * HOPS + HOPS - 1, OWN_AT + kind)
        )
        h = jnp.where(
            is_end,
            jnp.where(is_x3, since - 6, jnp.where(since >= 3, 1, 0)),
            jnp.where(is_own, lax.div(i, 2), lax.rem(i, 2)),
        )

        @pl.when(is_x)
        def _():
            for k in range(PIECES // HALVES):
                j = h * (PIECES // HALVES) + k
                x_copy(x_slot, j, buf.at[X_AT, piece(j)], sibling).wait_recv()

        @pl.when(jnp.logical_or(is_end, i < 8))
        def _():
            visit(slot, h, kind, is_own)

        return 0

    lax.fori_loop(0, ending + 8, turn, 0)
    finish(core)
    loss_ref[...] = jnp.sum(loss_acc[...].T, axis=0, keepdims=True) / (4.0 * rows_here)

    def drain(j, _):
        for slot in range(4):
            x_copy(slot, j, buf.at[X_AT, piece(j)], sibling).wait_send()
        for kind in (TXT, IMG):
            n = sends - PIECES + j
            ring_copy(kind, n, landing(kind, n)).wait_send()
        return 0

    lax.fori_loop(0, PIECES, drain, 0)


def hand_out(grads_ref, loss_in, img_out, txt_out, loss_out, sems):
    copies = [
        pltpu.make_async_copy(grads_ref.at[one], out, sems.at[one])
        for one, out in ((TXT, img_out), (IMG, txt_out))
    ]
    for copy in copies:
        copy.start()
    loss_out[...] = loss_in[...]
    for copy in copies:
        copy.wait()


def solution(mesh):
    n_gx, n_gy = mesh.shape["gx"], mesh.shape["gy"]

    def body(img, txt, scale, offset):
        rows, width = img.shape
        half = rows // HALVES
        sends = HOPS * PIECES

        def run(*refs):
            kernel(n_gx, n_gy, *refs)

        any_space = pl.BlockSpec(memory_space=pl.ANY)
        smem = pl.BlockSpec(memory_space=pltpu.SMEM)
        vmem = pl.BlockSpec(memory_space=pltpu.VMEM)
        grads, loss = pl.pallas_call(
            run,
            out_shape=(pltpu.VMEM((2, rows, width), BF16), pltpu.VMEM((1, rows), F32)),
            in_specs=[any_space, any_space, smem, smem],
            out_specs=(vmem, vmem),
            scratch_shapes=[
                pltpu.VMEM((N_SLOTS, rows, width), BF16),
                pltpu.VMEM((2, rows, width), BF16),
                pltpu.VMEM((2, rows, width), F32),
                pltpu.VMEM((rows, half // 2), F32),
                pltpu.VMEM((half, width), BF16),
                pltpu.VMEM((rows, half), F32),
                pltpu.VMEM((rows, half), BF16),
                pltpu.SemaphoreType.DMA((2, SEMS)),
                pltpu.SemaphoreType.DMA((2, sends)),
                pltpu.SemaphoreType.DMA((4, PIECES)),
                pltpu.SemaphoreType.DMA((4, PIECES)),
                pltpu.SemaphoreType.DMA((2,)),
            ],
            compiler_params=pltpu.CompilerParams(
                collective_id=0, has_side_effects=True, vmem_limit_bytes=52 * 1024 * 1024
            ),
            cost_estimate=pl.CostEstimate(
                flops=14 * 2 * rows * rows * width, bytes_accessed=8 * rows * width, transcendentals=0
            ),
        )(img, txt, scale, offset)
        img_grad, txt_grad, loss = pl.pallas_call(
            hand_out,
            out_shape=(
                jax.ShapeDtypeStruct((rows, width), BF16),
                jax.ShapeDtypeStruct((rows, width), BF16),
                jax.ShapeDtypeStruct((1, rows), F32),
            ),
            in_specs=[vmem, vmem],
            out_specs=(any_space, any_space, vmem),
            scratch_shapes=[pltpu.SemaphoreType.DMA((2,))],
            compiler_params=pltpu.CompilerParams(vmem_limit_bytes=4 * 1024 * 1024),
        )(grads, loss)
        return loss.reshape(rows), img_grad, txt_grad

    return jax.shard_map(
        body,
        mesh=mesh,
        in_specs=(P(("gx", "gy"), None), P(("gx", "gy"), None), P(), P()),
        out_specs=(P(("gx", "gy")), P(("gx", "gy"), None), P(("gx", "gy"), None)),
        check_vma=False,
    )
```

time: 249 us -> 238 us (0.956)
  Pallas kernels: 244 us -> 234 us
    pallas_call x1, Pallas kernels: 240 us -> 232 us  [body(): pl.pallas_call(run, out_shape=(pltpu.VMEM((2, rows, width), BF16), pltpu....]
where the time goes in v3:
time: 238 us; the launch traced here: 236 us
  Pallas kernels  234 us (98%)
    pallas_call x1, Pallas kernels, body(): pl.pallas_call(run, out_shape=(pltpu.VMEM((2, rows, width), BF16), pltpu....  232 us

profile of v3, /device:TPU:1, one launch (start us, length us, event | category | flops | bytes accessed | tf_op | source)
XLA Modules:
  0.0 236.1 jit_solution(13215468602315109716)
XLA Ops:
  1.9 232.2 %shard_map.67 = (bf16[2,512,1152]{2,1,0:T(8,128)(2,1)S(1)}, f32[1,512]{1,0:T(1,128)S(1)}) custom-call(bf16[512,1152]{1,0:T(8,128)(2,1)} %refs_0_.1, bf16[512,1152]{1,0:T(8,128)(2,1)} %refs_1_.1, f32[1]{0:T(128)S(6)} %copy.7.refs_2_, f32[1]{0:T(128)S(6)} %copy.8.refs_3_), custom_call_target="tpu_custom_call" | custom-call | flops 8455716864 | bytes 4718592 | tf_op jit(solution)/shard_map/pallas_call | solution.py:323
  234.1 2.0 shard_map.68

commit v4 on v3

--- a/solution.py
+++ b/solution.py
@@ -38,6 +38,7 @@
     block,
     scores,
     coef,
+    own_inv,
     ring_send,
     ring_recv,
     x_send,
@@ -113,17 +114,19 @@
         for kind in (TXT, IMG):
             ring_copy(kind, n, inputs[kind].at[piece(n)]).start()
 
-    def unit(raw):
-        wide = raw.astype(F32)
-        return wide * lax.rsqrt(jnp.sum(wide * wide, axis=-1, keepdims=True) + 1e-06)
+    def inverse_of(wide):
+        return lax.rsqrt(jnp.sum(wide * wide, axis=-1, keepdims=True) + 1e-06)
 
     def normalize_own(kind):
         def some_rows(i, _):
             at = pl.ds(pl.multiple_of(i * FIN_ROWS, FIN_ROWS), FIN_ROWS)
-            own_n[kind, at] = unit(buf[OWN_AT + kind, at]).astype(BF16)
+            wide = buf[OWN_AT + kind, at].astype(F32)
+            inverse = inverse_of(wide)
+            own_inv[kind, at] = inverse
+            own_n[kind, at] = (wide * inverse).astype(BF16)
             return 0
 
-        lax.fori_loop(0, rows_here // FIN_ROWS, some_rows, 0)
+        lax.fori_loop(0, rows_here // FIN_ROWS, some_rows, 0, unroll=4)
 
     set_out(0)
     own_loads = [
@@ -132,12 +135,12 @@
     ]
     for load in own_loads:
         load.start()
-    scale, offset = scale_ref[0], offset_ref[0]
     acc[...] = jnp.zeros_like(acc)
     loss_acc[...] = jnp.zeros_like(loss_acc)
     set_out(1)
     for load in own_loads:
         load.wait()
+    scale, offset = scale_ref[0], offset_ref[0]
     normalize_own(TXT)
     set_out(2)
     normalize_own(IMG)
@@ -154,9 +157,11 @@
                 drive = jnp.where(match, -drive, drive)
                 weight = jnp.where(match, -scale, scale)
             power = jnp.exp(drive)
-            coef[at] = (weight * (power * (1.0 / (1.0 + power)))).astype(BF16)
+            whole = 1.0 + power
+            rough = pl.reciprocal(whole, approx=True)
+            coef[at] = (weight * power * (rough * (2.0 - whole * rough))).astype(BF16)
             if with_loss:
-                loss = jnp.log1p(power)
+                loss = jnp.log(whole)
                 fold = half // 2
                 loss_acc[at] += loss[:, :fold] + loss[:, fold:]
             return 0
@@ -167,7 +172,8 @@
         def some_rows(i, _):
             at = pl.ds(pl.multiple_of(h * half + i * FIN_ROWS, FIN_ROWS), FIN_ROWS)
             to = pl.ds(pl.multiple_of(i * FIN_ROWS, FIN_ROWS), FIN_ROWS)
-            block[to] = unit(buf[slot, at]).astype(BF16)
+            wide = buf[slot, at].astype(F32)
+            block[to] = (wide * inverse_of(wide)).astype(BF16)
             return 0
 
         lax.fori_loop(0, half // FIN_ROWS, some_rows, 0, unroll=4)
@@ -195,7 +201,7 @@
             at = pl.ds(pl.multiple_of(i * FIN_ROWS, FIN_ROWS), FIN_ROWS)
             direction = acc[kind, at]
             raw = buf[OWN_AT + 1 - kind, at].astype(F32)
-            inverse = lax.rsqrt(jnp.sum(raw * raw, axis=-1, keepdims=True) + 1e-06)
+            inverse = own_inv[1 - kind, at]
             along = jnp.sum(raw * direction, axis=-1, keepdims=True) * (inverse * inverse * inverse)
             grads_ref[kind, at] = (inverse * direction - along * raw).astype(BF16)
             return 0
@@ -204,6 +210,14 @@
 
     def within(i, low, count):
         return jnp.logical_and(i >= low, i < low + count)
+
+    def drain(j, _):
+        for slot in range(4):
+            x_copy(slot, j, buf.at[X_AT, piece(j)], sibling).wait_send()
+        for kind in (TXT, IMG):
+            n = sends - PIECES + j
+            ring_copy(kind, n, landing(kind, n)).wait_send()
+        return 0
 
     ending = sends - 3
 
@@ -246,6 +260,7 @@
         @pl.when(since == 7)
         def _():
             finish(1 - core)
+            lax.fori_loop(0, PIECES, drain, 0)
 
         is_end = since >= 0
         is_own = i < 4
@@ -282,16 +297,6 @@
     lax.fori_loop(0, ending + 8, turn, 0)
     finish(core)
     loss_ref[...] = jnp.sum(loss_acc[...].T, axis=0, keepdims=True) / (4.0 * rows_here)
-
-    def drain(j, _):
-        for slot in range(4):
-            x_copy(slot, j, buf.at[X_AT, piece(j)], sibling).wait_send()
-        for kind in (TXT, IMG):
-            n = sends - PIECES + j
-            ring_copy(kind, n, landing(kind, n)).wait_send()
-        return 0
-
-    lax.fori_loop(0, PIECES, drain, 0)
 
 
 def hand_out(grads_ref, loss_in, img_out, txt_out, loss_out, sems):
@@ -333,6 +338,7 @@
                 pltpu.VMEM((half, width), BF16),
                 pltpu.VMEM((rows, half), F32),
                 pltpu.VMEM((rows, half), BF16),
+                pltpu.VMEM((2, rows, 1), F32),
                 pltpu.SemaphoreType.DMA((2, SEMS)),
                 pltpu.SemaphoreType.DMA((2, sends)),
                 pltpu.SemaphoreType.DMA((4, PIECES)),

time: 238 us -> 239 us (level)
  Pallas kernels: 234 us -> 237 us
    pallas_call x1, Pallas kernels: 232 us -> 235 us  [body(): pl.pallas_call(run, out_shape=(pltpu.VMEM((2, rows, width), BF16), pltpu....]
where the time goes in v4:
time: 239 us
  Pallas kernels  237 us (99%)
    pallas_call x1, Pallas kernels, body(): pl.pallas_call(run, out_shape=(pltpu.VMEM((2, rows, width), BF16), pltpu....  235 us

profile of v4, /device:TPU:1, one launch (start us, length us, event | category | flops | bytes accessed | tf_op | source)
XLA Modules:
  0.0 238.8 jit_solution(4161720766367654876)
XLA Ops:
  1.9 234.9 %shard_map.67 = (bf16[2,512,1152]{2,1,0:T(8,128)(2,1)S(1)}, f32[1,512]{1,0:T(1,128)S(1)}) custom-call(bf16[512,1152]{1,0:T(8,128)(2,1)} %refs_0_.1, bf16[512,1152]{1,0:T(8,128)(2,1)} %refs_1_.1, f32[1]{0:T(128)S(6)} %copy.7.refs_2_, f32[1]{0:T(128)S(6)} %copy.8.refs_3_), custom_call_target="tpu_custom_call" | custom-call | flops 8455716864 | bytes 4718592 | tf_op jit(solution)/shard_map/pallas_call | solution.py:328
  236.8 2.0 shard_map.68

commit v5 on v3

--- a/solution.py
+++ b/solution.py
@@ -12,6 +12,7 @@
 TXT, IMG = 0, 1
 HOPS = 8
 PIECES = 4
+OWN_NINTH = 2
 HALVES = 2
 SEMS = 16
 SUB = 64
@@ -38,6 +39,9 @@
     block,
     scores,
     coef,
+    shared,
+    shared_send,
+    shared_recv,
     ring_send,
     ring_recv,
     x_send,
@@ -71,10 +75,19 @@
         jnp.where(core == 0, jnp.where(q == 0, last, q - 1), jnp.where(q == last, 0, q + 1)),
     )
 
+    shared_to = device(
+        jnp.where(core == 0, jnp.where(q == last - 1, gx(p - 1), p), jnp.where(q == 1, gx(p + 1), p)),
+        jnp.where(core == 0, jnp.where(q == last - 1, 0, q + 2), jnp.where(q == 1, last, q - 2)),
+    )
+    shared_from = device(
+        jnp.where(core == 0, jnp.where(q == 0, gx(p + 1), p), jnp.where(q == last, gx(p - 1), p)),
+        jnp.where(core == 0, jnp.where(q == 0, last - 1, q - 2), jnp.where(q == last, 1, q + 2)),
+    )
+
     barrier = pltpu.get_barrier_semaphore()
-    for source in (up, down, sibling, ninth_from):
+    for source in (up, down, sibling, ninth_from, shared_from):
         pl.semaphore_signal(barrier, inc=1, device_id=source, device_id_type=MESH)
-    pl.semaphore_wait(barrier, 4)
+    pl.semaphore_wait(barrier, 5)
 
     def piece(j):
         return pl.ds(pl.multiple_of(j * part, part), part)
@@ -104,6 +117,20 @@
             device_id=target,
             device_id_type=MESH,
         )
+
+    def to_share(k, src):
+        return pltpu.make_async_remote_copy(
+            src_ref=src,
+            dst_ref=shared.at[k],
+            send_sem=shared_send.at[k],
+            recv_sem=shared_recv.at[k],
+            device_id=sibling,
+            device_id_type=MESH,
+        )
+
+    def pass_shared(k):
+        to_share(k, shared.at[k]).wait_recv()
+        x_copy(3, k + OWN_NINTH, shared.at[k], shared_to).start()
 
     inputs = (txt_ref, img_ref)
     short = core
@@ -221,10 +248,14 @@
                 def _():
                     ring_copy(kind, onward, landing(kind, t)).start()
 
-                @pl.when(jnp.logical_and(onward >= sends, short != kind))
+                @pl.when(jnp.logical_and(within(onward, sends, OWN_NINTH), short != kind))
                 def _():
                     x_copy(3, j, landing(kind, t), ninth_to).start()
 
+                @pl.when(jnp.logical_and(onward >= sends + OWN_NINTH, short != kind))
+                def _():
+                    to_share(j - OWN_NINTH, landing(kind, t)).start()
+
                 @pl.when(jnp.logical_and(onward >= sends, short == kind))
                 def _():
                     x_copy(1, j, landing(kind, t), sibling).start()
@@ -242,6 +273,12 @@
                     ring_copy(kind, t - PIECES, landing(kind, t)).wait_send()
 
         since = i - ending
+
+        for k in range(PIECES - OWN_NINTH):
+
+            @pl.when(since == k + 3)
+            def _():
+                pass_shared(k)
 
         @pl.when(since == 7)
         def _():
@@ -282,6 +319,9 @@
     lax.fori_loop(0, ending + 8, turn, 0)
     finish(core)
     loss_ref[...] = jnp.sum(loss_acc[...].T, axis=0, keepdims=True) / (4.0 * rows_here)
+
+    for k in range(PIECES - OWN_NINTH):
+        to_share(k, shared.at[k]).wait_send()
 
     def drain(j, _):
         for slot in range(4):
@@ -333,6 +373,9 @@
                 pltpu.VMEM((half, width), BF16),
                 pltpu.VMEM((rows, half), F32),
                 pltpu.VMEM((rows, half), BF16),
+                pltpu.VMEM((PIECES - OWN_NINTH, rows // PIECES, width), BF16),
+                pltpu.SemaphoreType.DMA((PIECES - OWN_NINTH,)),
+                pltpu.SemaphoreType.DMA((PIECES - OWN_NINTH,)),
                 pltpu.SemaphoreType.DMA((2, SEMS)),
                 pltpu.SemaphoreType.DMA((2, sends)),
                 pltpu.SemaphoreType.DMA((4, PIECES)),

time: 238 us -> 238 us (level)
  no operation moved by 1% of the time
where the time goes in v5:
time: 238 us; the launch traced here: 236 us
  Pallas kernels  234 us (98%)
    pallas_call x1, Pallas kernels, body(): pl.pallas_call(run, out_shape=(pltpu.VMEM((2, rows, width), BF16), pltpu....  232 us

profile of v5, /device:TPU:1, one launch (start us, length us, event | category | flops | bytes accessed | tf_op | source)
XLA Modules:
  0.0 236.4 jit_solution(11773163708871062725)
XLA Ops:
  1.9 232.4 %shard_map.67 = (bf16[2,512,1152]{2,1,0:T(8,128)(2,1)S(1)}, f32[1,512]{1,0:T(1,128)S(1)}) custom-call(bf16[512,1152]{1,0:T(8,128)(2,1)} %refs_0_.1, bf16[512,1152]{1,0:T(8,128)(2,1)} %refs_1_.1, f32[1]{0:T(128)S(6)} %copy.7.refs_2_, f32[1]{0:T(128)S(6)} %copy.8.refs_3_), custom_call_target="tpu_custom_call" | custom-call | flops 8455716864 | bytes 4718592 | tf_op jit(solution)/shard_map/pallas_call | solution.py:363
  234.4 2.0 shard_map.68

commit v6 on v3

--- a/solution.py
+++ b/solution.py
@@ -143,10 +143,10 @@
     normalize_own(IMG)
     set_out(3)
 
-    def weigh(h, own_pair, with_loss):
+    def weigh(h, size, own_pair, with_loss):
         def some_rows(i, _):
             at = pl.ds(pl.multiple_of(i * SUB, SUB), SUB)
-            drive = scale * scores[at] + offset
+            drive = scale * scores[at, :size] + offset
             weight = scale
             if own_pair:
                 row = lax.broadcasted_iota(jnp.int32, drive.shape, 0) + i * SUB
@@ -154,41 +154,44 @@
                 drive = jnp.where(match, -drive, drive)
                 weight = jnp.where(match, -scale, scale)
             power = jnp.exp(drive)
-            coef[at] = (weight * (power * (1.0 / (1.0 + power)))).astype(BF16)
+            coef[at, :size] = (weight * (power * (1.0 / (1.0 + power)))).astype(BF16)
             if with_loss:
                 loss = jnp.log1p(power)
-                fold = half // 2
-                loss_acc[at] += loss[:, :fold] + loss[:, fold:]
+                loss_acc[at] += loss if size == part else loss[:, :part] + loss[:, part:]
             return 0
 
         lax.fori_loop(0, rows_here // SUB, some_rows, 0, unroll=2)
 
-    def visit(slot, h, kind, own_pair):
+    def visit(slot, h, size, kind, own_pair):
         def some_rows(i, _):
-            at = pl.ds(pl.multiple_of(h * half + i * FIN_ROWS, FIN_ROWS), FIN_ROWS)
+            at = pl.ds(pl.multiple_of(h * size + i * FIN_ROWS, FIN_ROWS), FIN_ROWS)
             to = pl.ds(pl.multiple_of(i * FIN_ROWS, FIN_ROWS), FIN_ROWS)
             block[to] = unit(buf[slot, at]).astype(BF16)
             return 0
 
-        lax.fori_loop(0, half // FIN_ROWS, some_rows, 0, unroll=4)
+        lax.fori_loop(0, size // FIN_ROWS, some_rows, 0, unroll=min(4, size // FIN_ROWS))
         for r in range(HALVES):
             at = pl.ds(r * half, half)
-            scores[at] = lax.dot_general(
-                own_n[1 - kind, at], block[...], (((1,), (1,)), ((), ())), preferred_element_type=F32
+            scores[at, :size] = lax.dot_general(
+                own_n[1 - kind, at],
+                block[:size],
+                (((1,), (1,)), ((), ())),
+                preferred_element_type=F32,
             )
         for one in (TXT, IMG):
-
-            @pl.when(jnp.logical_and(own_pair, kind == one))
-            def _():
-                weigh(h, True, one == TXT)
+            if own_pair is not False:
+
+                @pl.when(jnp.logical_and(own_pair, kind == one))
+                def _():
+                    weigh(h, size, True, one == TXT)
 
             @pl.when(jnp.logical_and(jnp.logical_not(own_pair), kind == one))
             def _():
-                weigh(h, False, one == TXT)
+                weigh(h, size, False, one == TXT)
 
         for r in range(HALVES):
             at = pl.ds(r * half, half)
-            acc[kind, at] += jnp.dot(coef[at], block[...], preferred_element_type=F32)
+            acc[kind, at] += jnp.dot(coef[at, :size], block[:size], preferred_element_type=F32)
 
     def finish(kind):
         def some_rows(i, _):
@@ -205,6 +208,14 @@
     def within(i, low, count):
         return jnp.logical_and(i >= low, i < low + count)
 
+    def drain(j, _):
+        for slot in range(3):
+            x_copy(slot, j, buf.at[X_AT, piece(j)], sibling).wait_send()
+        for kind in (TXT, IMG):
+            n = sends - PIECES + j
+            ring_copy(kind, n, landing(kind, n)).wait_send()
+        return 0
+
     ending = sends - 3
 
     def turn(i, _):
@@ -246,6 +257,7 @@
         @pl.when(since == 7)
         def _():
             finish(1 - core)
+            lax.fori_loop(0, PIECES, drain, 0)
 
         is_end = since >= 0
         is_own = i < 4
@@ -267,36 +279,39 @@
             jnp.where(is_own, lax.div(i, 2), lax.rem(i, 2)),
         )
 
-        @pl.when(is_x)
+        @pl.when(jnp.logical_and(is_x, since <= 6))
         def _():
             for k in range(PIECES // HALVES):
                 j = h * (PIECES // HALVES) + k
                 x_copy(x_slot, j, buf.at[X_AT, piece(j)], sibling).wait_recv()
 
-        @pl.when(jnp.logical_or(is_end, i < 8))
-        def _():
-            visit(slot, h, kind, is_own)
+        @pl.when(jnp.logical_or(within(since, 0, 7), i < 8))
+        def _():
+            visit(slot, h, half, kind, is_own)
+
+        @pl.when(since >= 7)
+        def _():
+            j = since - 7 + PIECES // HALVES
+            x_copy(3, j, buf.at[X_AT, piece(j)], sibling).wait_recv()
+            visit(X_AT + 3, j, part, core, False)
 
         return 0
 
-    lax.fori_loop(0, ending + 8, turn, 0)
+    lax.fori_loop(0, ending + 7 + PIECES // HALVES, turn, 0)
     finish(core)
     loss_ref[...] = jnp.sum(loss_acc[...].T, axis=0, keepdims=True) / (4.0 * rows_here)
 
-    def drain(j, _):
-        for slot in range(4):
-            x_copy(slot, j, buf.at[X_AT, piece(j)], sibling).wait_send()
-        for kind in (TXT, IMG):
-            n = sends - PIECES + j
-            ring_copy(kind, n, landing(kind, n)).wait_send()
-        return 0
-
-    lax.fori_loop(0, PIECES, drain, 0)
+    for j in range(PIECES):
+        x_copy(3, j, buf.at[X_AT, piece(j)], sibling).wait_send()
 
 
 def hand_out(grads_ref, loss_in, img_out, txt_out, loss_out, sems):
+    part = img_out.shape[0] // PIECES
     copies = [
-        pltpu.make_async_copy(grads_ref.at[one], out, sems.at[one])
+        pltpu.make_async_copy(
+            grads_ref.at[one, pl.ds(j * part, part)], out.at[pl.ds(j * part, part)], sems.at[one, j]
+        )
+        for j in range(PIECES)
         for one, out in ((TXT, img_out), (IMG, txt_out))
     ]
     for copy in copies:
@@ -355,7 +370,7 @@
             ),
             in_specs=[vmem, vmem],
             out_specs=(any_space, any_space, vmem),
-            scratch_shapes=[pltpu.SemaphoreType.DMA((2,))],
+            scratch_shapes=[pltpu.SemaphoreType.DMA((2, PIECES))],
             compiler_params=pltpu.CompilerParams(vmem_limit_bytes=4 * 1024 * 1024),
         )(grads, loss)
         return loss.reshape(rows), img_grad, txt_grad

time: 238 us -> 238 us (level)
  no operation moved by 1% of the time
where the time goes in v6:
time: 238 us; the launch traced here: 236 us
  Pallas kernels  234 us (98%)
    pallas_call x1, Pallas kernels, body(): pl.pallas_call(run, out_shape=(pltpu.VMEM((2, rows, width), BF16), pltpu....  232 us

profile of v6, /device:TPU:1, one launch (start us, length us, event | category | flops | bytes accessed | tf_op | source)
XLA Modules:
  0.0 236.1 jit_solution(10488782911480672547)
XLA Ops:
  1.9 232.2 %shard_map.67 = (bf16[2,512,1152]{2,1,0:T(8,128)(2,1)S(1)}, f32[1,512]{1,0:T(1,128)S(1)}) custom-call(bf16[512,1152]{1,0:T(8,128)(2,1)} %refs_0_.1, bf16[512,1152]{1,0:T(8,128)(2,1)} %refs_1_.1, f32[1]{0:T(128)S(6)} %copy.7.refs_2_, f32[1]{0:T(128)S(6)} %copy.8.refs_3_), custom_call_target="tpu_custom_call" | custom-call | flops 8455716864 | bytes 4718592 | tf_op jit(solution)/shard_map/pallas_call | solution.py:338
  234.1 2.0 shard_map.68

commit v7 on v6

--- a/solution.py
+++ b/solution.py
@@ -125,7 +125,8 @@
 
         lax.fori_loop(0, rows_here // FIN_ROWS, some_rows, 0)
 
-    set_out(0)
+    for n in range(PIECES):
+        set_out(n)
     own_loads = [
         pltpu.make_async_copy(inputs[kind], buf.at[OWN_AT + kind], local_sem.at[kind])
         for kind in (TXT, IMG)
@@ -135,13 +136,10 @@
     scale, offset = scale_ref[0], offset_ref[0]
     acc[...] = jnp.zeros_like(acc)
     loss_acc[...] = jnp.zeros_like(loss_acc)
-    set_out(1)
     for load in own_loads:
         load.wait()
     normalize_own(TXT)
-    set_out(2)
     normalize_own(IMG)
-    set_out(3)
 
     def weigh(h, size, own_pair, with_loss):
         def some_rows(i, _):

time: 238 us -> 238 us (level)
  no operation moved by 1% of the time
where the time goes in v7:
time: 238 us; the launch traced here: 236 us
  Pallas kernels  234 us (98%)
    pallas_call x1, Pallas kernels, body(): pl.pallas_call(run, out_shape=(pltpu.VMEM((2, rows, width), BF16), pltpu....  232 us

profile of v7, /device:TPU:1, one launch (start us, length us, event | category | flops | bytes accessed | tf_op | source)
XLA Modules:
  0.0 236.1 jit_solution(340032365853119545)
XLA Ops:
  1.9 232.2 %shard_map.67 = (bf16[2,512,1152]{2,1,0:T(8,128)(2,1)S(1)}, f32[1,512]{1,0:T(1,128)S(1)}) custom-call(bf16[512,1152]{1,0:T(8,128)(2,1)} %refs_0_.1, bf16[512,1152]{1,0:T(8,128)(2,1)} %refs_1_.1, f32[1]{0:T(128)S(6)} %copy.7.refs_2_, f32[1]{0:T(128)S(6)} %copy.8.refs_3_), custom_call_target="tpu_custom_call" | custom-call | flops 8455716864 | bytes 4718592 | tf_op jit(solution)/shard_map/pallas_call | solution.py:336
  234.1 2.0 shard_map.68
